TPU v7x, 32 devices: a whole 2x2x4 slice. The times are simulated.
32 devices in a mesh: chan: 8 (over y, x, core), freq: 4 (over z), win: 1.
Axes of the slice: x: 2, y: 2, z: 4, core: 2. Of those that a mesh axis runs over, the one named last changes fastest.
Arguments:
- rec_block: bfloat16 [12, 32, 6000], P('win', ('chan', 'freq')), may hold values from -70 to 70
- rec_partner: bfloat16 [12, 128, 6000], P('win', ('chan', 'freq')), may hold values from -70 to 70
- flag_block: int32 [12, 32], P('win', ('chan', 'freq')), may hold values 0 or 1
- flag_partner: int32 [12, 128], P('win', ('chan', 'freq')), may hold values 0 or 1
Outputs:
- cross: float32 [2, 512, 32, 128], P(None, 'freq', 'chan', 'win')
All inputs are finite; a program needn't handle non-finite values. No bound on the sum of `flag_block` or of `flag_partner` on one device may be relied on, other than what follows from the above.
Results may differ from a plain program's by a relative error of at most 0.0059.
Values may be sent and summed in bfloat16 or wider, within the bound.
A program may use at most 64 MiB of HBM per device.

v0:
```python
import math

import jax
import jax.numpy as jnp
from jax import lax
from jax.sharding import PartitionSpec as P

F = 512
FLO = 60


def harmonic_kernel_grid(reading_moments, spectral_slots, reading_offsets):
    cycle_offset = reading_moments[:, None] * spectral_slots[None, :] % reading_offsets
    cycle_radians = cycle_offset.astype(jnp.float32) * (2.0 * math.pi / reading_offsets)
    return jnp.concatenate([jnp.cos(cycle_radians), -jnp.sin(cycle_radians)], axis=1).astype(
        jnp.bfloat16
    )


def transform(records):
    reading_offsets = records.shape[1]
    extent_count = reading_offsets // 4
    spectral_slots = jnp.arange(F, dtype=jnp.int32) + FLO
    accumulated = jnp.zeros((records.shape[0], 2 * F), jnp.float32)
    for cosine_lag in range(4):
        reading_moments = jnp.arange(extent_count, dtype=jnp.int32) + cosine_lag * extent_count
        harmonic_operator = harmonic_kernel_grid(reading_moments, spectral_slots, reading_offsets)
        accumulated = accumulated + jnp.dot(
            records[:, cosine_lag * extent_count : (cosine_lag + 1) * extent_count],
            harmonic_operator,
            preferred_element_type=jnp.float32,
        )
    return accumulated


def rotate(whitened):
    turned = jnp.concatenate([whitened[:, 1:2], -whitened[:, 0:1]], axis=1)
    return jnp.stack([whitened, turned])


def body(rec_block, rec_partner, flag_block, flag_partner):
    windows, block_dev, reading_offsets = rec_block.shape
    partner_dev = rec_partner.shape[1]
    channels = block_dev + partner_dev
    records = jnp.concatenate([rec_block, rec_partner], axis=1).reshape(
        windows * channels, reading_offsets
    )
    spectra = transform(records).reshape(windows, channels, 2, F)
    band_power = jnp.sum(spectra * spectra, axis=(2, 3), keepdims=True) / F
    quality = jnp.concatenate([flag_block, flag_partner], axis=1).astype(jnp.float32)[
        :, :, None, None
    ]
    whitened = (quality * spectra * lax.rsqrt(band_power + 1e-06)).astype(jnp.bfloat16)
    whitened = jnp.transpose(whitened, (0, 2, 1, 3))
    block_white = whitened[:, :, :block_dev]
    partner_white = whitened[:, :, block_dev:]
    block_white, partner_white = (
        lax.all_to_all(block_white, "freq", split_axis=3, concat_axis=2, tiled=True),
        lax.all_to_all(partner_white, "freq", split_axis=3, concat_axis=2, tiled=True),
    )
    stack_scale = 1.0 / math.sqrt(windows * lax.axis_size("win"))
    paired = rotate(block_white)
    partials = jnp.einsum(
        "owsaf,wsbf->ofab",
        paired,
        lax.all_gather(partner_white, "chan", axis=2, tiled=True),
        preferred_element_type=jnp.float32,
    )
    summed = lax.psum_scatter(partials, "win", scatter_dimension=3, tiled=True)
    return summed * stack_scale


def solution(mesh):
    placed = (
        P("win", ("chan", "freq"), None),
        P("win", ("chan", "freq"), None),
        P("win", ("chan", "freq")),
        P("win", ("chan", "freq")),
    )
    return jax.shard_map(
        body, mesh=mesh, in_specs=placed, out_specs=P(None, "freq", "chan", "win"), check_vma=False
    )
```

profile of v0, /device:TPU:1, one launch (start us, length us, event | category | flops | bytes accessed | tf_op | source)
XLA Modules:
  0.0 104.1 jit_solution(15057867350134833870)
XLA Ops:
  0.0 1.2 %copy.28 = bf16[12,1,6000]{2,1,0:T(2,128)(2,1)S(1)} copy(bf16[12,1,6000]{2,0,1:T(8,128)(2,1)} %param.4) | data formatting | bytes 288000 | tf_op args[0]
  1.2 1.6 %pad_maximum_fusion = bf16[12,5,6000]{2,1,0:T(8,128)(2,1)S(1)} fusion(bf16[12,4,6000]{2,1,0:T(4,128)(2,1)} %param.5, bf16[12,1,6000]{2,1,0:T(2,128)(2,1)S(1)} %copy.28), kind=kLoop, calls=%fused_computation.60 | loop fusion | flops 1440000 | bytes 1440000 | tf_op jit(solution)/shard_map/concatenate | solution.py:45
  2.8 0.5 reshape.59
  3.3 51.8 %cosine_convert_fusion = (bf16[1500,512]{1,0:T(8,128)(2,1)S(1)}, bf16[1500,512]{1,0:T(8,128)(2,1)S(1)}, bf16[1500,512]{1,0:T(8,128)(2,1)S(1)}, bf16[1500,512]{1,...) fusion(s32[1500]{0:T(1024)S(1)} %get-tuple-element.21, ...), kind=kLoop, calls=%fused_computation.30 | loop fusion | flops 36864000 | bytes 12308048 | tf_op jit(solution)/shard_map/convert
  55.1 0.7 fusion.8
  55.8 0.7 fusion.45
  56.5 0.7 fusion.42
  57.2 0.8 multiply_reduce_fusion
  58.0 0.0 copy-start
  58.0 0.0 copy-start.1
  58.0 0.1 rsqrt.12
  58.1 0.1 copy.30
  58.2 0.2 reshape.60
  58.4 3.7 %copy.29 = f32[12,5,2,512]{0,1,2,3:T(8,128)} copy(f32[12,5,2,512]{3,2,1,0:T(2,128)S(1)} %reshape.60) | data formatting | bytes 491520 | tf_op jit(solution)/shard_map/reshape | solution.py:48
  62.1 0.0 copy-done
  62.1 0.0 copy-done.1
  62.1 2.6 %fusion.36 = bf16[12,2,5,512]{0,2,1,3:T(8,128)(2,1)S(1)} fusion(f32[12,5,2,512]{0,1,2,3:T(8,128)} %copy.29, f32[12,5]{0,1:T(8,128)S(1)} %copy.30, f32[12,5]{0,1:T(8,128)S(1)} %add_convert_fusion), kind=kLoop, calls=%fused_computation.53 | loop fusion | flops 184320 | bytes 369120 | tf_op jit(solution)/shard_map/transpose | solution.py:54
  64.7 0.4 slice.37
  65.1 0.2 copy.48
  65.3 1.0 reshape.65
  66.3 5.4 %all-to-all-start.1 = ((bf16[4,2,1536]{2,1,0:T(2,128)(2,1)}), bf16[4,2,1536]{2,1,0:T(2,128)(2,1)S(1)}, u32[]{:S(2)}, u32[]{:S(2)}) async-start(bf16[4,2,1536]{2,1,0:T(2,128)(2,1)} %reshape.65), calls=%async_computation.1 | async-start | bytes 49152 | tf_op jit(solution)/shard_map/all_to_all | solution.py:58
  71.7 0.6 slice_bitcast_fusion
  72.3 2.7 %reshape.63 = bf16[4,2,6144]{2,1,0:T(2,128)(2,1)} reshape(bf16[512,2,4,12]{3,2,1,0:T(4,128)(2,1)S(1)} %slice_bitcast_fusion) | data formatting | bytes 196608
  75.0 1.2 %all-to-all-done.1 = bf16[4,2,1536]{2,1,0:T(2,128)(2,1)S(1)} async-done(((bf16[4,2,1536]{2,1,0:T(2,128)(2,1)}), bf16[4,2,1536]{2,1,0:T(2,128)(2,1)S(1)}, u32[]{:S(2)}, u32[]{:S(2)}) %all-to-all-start.1) | async-done | bytes 24608 | tf_op jit(solution)/shard_map/all_to_all | solution.py:58
  76.2 3.3 %all-to-all-start = ((bf16[4,2,6144]{2,1,0:T(2,128)(2,1)}), bf16[4,2,6144]{2,1,0:T(2,128)(2,1)S(1)}, u32[]{:S(2)}, u32[]{:S(2)}) async-start(bf16[4,2,6144]{2,1,0:T(2,128)(2,1)} %reshape.63), calls=%async_computation | async-start | bytes 196608 | tf_op jit(solution)/shard_map/all_to_all | solution.py:59
  79.5 0.6 reshape.66
  80.1 0.4 fusion.56
  80.5 0.1 copy.45
  80.6 0.1 copy.46
  80.8 0.2 copy.43
  81.0 0.5 copy.37
  81.5 2.7 %all-to-all-done = bf16[4,2,6144]{2,1,0:T(2,128)(2,1)S(1)} async-done(((bf16[4,2,6144]{2,1,0:T(2,128)(2,1)}), bf16[4,2,6144]{2,1,0:T(2,128)(2,1)S(1)}, u32[]{:S(2)}, u32[]{:S(2)}) %all-to-all-start) | async-done | bytes 98336 | tf_op jit(solution)/shard_map/all_to_all | solution.py:59
  84.2 2.4 %reshape.64 = bf16[512,2,4,12]{3,2,1,0:T(4,128)(2,1)S(1)} reshape(bf16[4,2,6144]{2,1,0:T(2,128)(2,1)S(1)} %all-to-all-done) | data formatting | bytes 196608
  86.6 0.9 copy.31
  87.5 0.1 copy.32
  87.6 13.5 %all_gather.3 = bf16[12,2,128,128]{3,1,0,2:T(2,128)(2,1)S(1)} all-gather(bf16[12,2,16,128]{3,1,0,2:T(2,128)(2,1)S(1)} %copy.32), channel_id=1, replica_groups=mesh['chan'=8,'freq'=4,'win'=1] {'chan'}, dimensions={2}, use_global_device_ids=true | all-gather | bytes 884736 | tf_op jit(solution)/shard_map/all_gather | solution.py:66
  101.1 1.7 %copy.39 = bf16[12,2,128,128,1]{2,0,1,4,3:T(8,128)(2,1)S(1)} copy(bf16[12,2,128,128,1]{3,1,0,2,4:T(2,128)(2,1)S(1)} %bitcast.32) | data formatting | bytes 1572864 | tf_op jit(solution)/shard_map/all_gather | solution.py:66
  102.7 0.5 fusion.38
  103.2 0.9 copy.38
  (8 shorter events, 0.1 us)
Async XLA Ops:
  58.0 4.1 %copy-start = (s32[12,4]{0,1:T(4,128)S(1)}, s32[12,4]{0,1:T(4,128)}, u32[]{:S(2)}) copy-start(s32[12,4]{0,1:T(4,128)} %param.7) | copy-start | bytes 580
  58.0 4.1 %copy-start.1 = (s32[12,1]{0,1:T(1,128)S(1)}, s32[12,1]{0,1:T(1,128)}, u32[]{:S(2)}) copy-start(s32[12,1]{0,1:T(1,128)} %param.6) | copy-start | bytes 148
  66.3 9.9 %all-to-all-start.1 = ((bf16[4,2,1536]{2,1,0:T(2,128)(2,1)}), bf16[4,2,1536]{2,1,0:T(2,128)(2,1)S(1)}, u32[]{:S(2)}, u32[]{:S(2)}) async-start(bf16[4,2,1536]{2,1,0:T(2,128)(2,1)} %reshape.65), calls=%async_computation.1 | async-start | bytes 49152 | tf_op jit(solution)/shard_map/all_to_all | solution.py:58
  76.2 8.0 %all-to-all-start = ((bf16[4,2,6144]{2,1,0:T(2,128)(2,1)}), bf16[4,2,6144]{2,1,0:T(2,128)(2,1)S(1)}, u32[]{:S(2)}, u32[]{:S(2)}) async-start(bf16[4,2,6144]{2,1,0:T(2,128)(2,1)} %reshape.63), calls=%async_computation | async-start | bytes 196608 | tf_op jit(solution)/shard_map/all_to_all | solution.py:59
where the time goes:
time: 105 us; the launch traced here: 104 us
  other arithmetic  56.2 us (54%)
  local copies, waits for them, and re-layouts  18.3 us (17%)
  blocking collectives  13.5 us (13%)
  starting transfers between devices  8.73 us (8%)
  waiting for transfers between devices  3.94 us (4%)
  matrix products  3.31 us (3%)
    another operation x1, other arithmetic  51.8 us
    all_gather x1, blocking collectives, body(): lax.all_gather(partner_white, 'chan', axis=2, tiled=True)  13.5 us
    unnamed x12, local copies, waits for them, and re-layouts  8.7 us
    all_to_all x1, starting transfers between devices, body(): lax.all_to_all(block_white, 'freq', split_axis=3, concat_axis=2, tiled=True)  5.42 us
    reshape x2, local copies, waits for them, and re-layouts, body(): spectra = transform(records).reshape(windows, channels, 2, F)  3.86 us
    all_to_all x1, starting transfers between devices, body(): lax.all_to_all(partner_white, 'freq', split_axis=3, concat_axis=2, tiled=...  3.32 us
    dot_general x4, matrix products, transform(): jnp.dot(records[:, cosine_lag * extent_count:(cosine_lag + 1) * extent_co...  2.86 us
    all_to_all x1, waiting for transfers between devices, body(): lax.all_to_all(partner_white, 'freq', split_axis=3, concat_axis=2, tiled=...  2.72 us
  transfers between devices with their start and end apart: 2, of which 2 were waited for; matrix products, arithmetic and copies ran while one was open for 5% of the time, Pallas kernels for 0%

commit v1 on v0

--- a/solution.py
+++ b/solution.py
@@ -1,8 +1,13 @@
+import functools
 import math
 
 import jax
 import jax.numpy as jnp
+import ml_dtypes
+import numpy as np
 from jax import lax
+from jax.experimental import pallas as pl
+from jax.experimental.pallas import tpu as pltpu
 from jax.sharding import PartitionSpec as P
 
 F = 512
@@ -70,6 +75,219 @@
     return summed * stack_scale
 
 
+MESH = pl.DeviceIdType.MESH
+LANES = 128
+DIRECT = (1, 2, 4, 6)
+
+
+def basis_table(samples):
+    s = np.arange(samples, dtype=np.int64)[:, None]
+    k = np.arange(F, dtype=np.int64)[None, :] + FLO
+    phase = (s * k % samples).astype(np.float64) * (2.0 * np.pi / samples)
+    return np.concatenate([np.cos(phase), -np.sin(phase)], axis=1).astype(ml_dtypes.bfloat16)
+
+
+def flip(chan, d):
+    core, x, y = chan % 2, (chan // 2) % 2, chan // 4
+    core = 1 - core if d & 1 else core
+    x = 1 - x if d & 2 else x
+    y = 1 - y if d & 4 else y
+    return core + 2 * x + 4 * y
+
+
+def kernel(
+    chunks, scale,
+    blk_hbm, par_hbm, fb_ref, fp_ref, basis_hbm, out_ref,
+    blk, par, basis, xs, slabs, zbuf, gath, coef, res,
+    load_sem, basis_sem, z_send, z_recv, p_send, p_recv,
+):
+    chan, z, win = lax.axis_index("chan"), lax.axis_index("freq"), lax.axis_index("win")
+    nwin = blk.shape[0]
+
+    blk_in = pltpu.make_async_copy(blk_hbm, blk, load_sem.at[0])
+    par_in = pltpu.make_async_copy(par_hbm, par, load_sem.at[1])
+    blk_in.start()
+    par_in.start()
+    loads = []
+    for i, (low, size) in enumerate(chunks):
+        rows = pl.ds(low, size)
+        load = pltpu.make_async_copy(basis_hbm.at[rows], basis.at[rows], basis_sem.at[i])
+        load.start()
+        loads.append(load)
+
+    barrier = pltpu.get_barrier_semaphore()
+    for r in (1, 2, 3):
+        pl.semaphore_signal(barrier, inc=1, device_id=(chan, (z + r) % 4, win), device_id_type=MESH)
+    for d in DIRECT:
+        pl.semaphore_signal(barrier, inc=1, device_id=(flip(chan, d), z, win), device_id_type=MESH)
+
+    par_in.wait()
+    for w in range(nwin):
+        xs[w * 4 : w * 4 + 4, :] = par[w].astype(jnp.float32)
+    blk_in.wait()
+    top = nwin * 4
+    xs[top : top + nwin, :] = blk[...].astype(jnp.float32)
+    xs[top + nwin :, :] = jnp.zeros((xs.shape[0] - top - nwin, xs.shape[1]), jnp.float32)
+
+    spec = None
+    for load, (low, size) in zip(loads, chunks):
+        load.wait()
+        x = xs[:, low : low + size].astype(jnp.bfloat16)
+        term = jnp.dot(x, basis[low : low + size, :], preferred_element_type=jnp.float32)
+        spec = term if spec is None else spec + term
+
+    power = jnp.sum(spec * spec, axis=1, keepdims=True) * (1.0 / F)
+    quality = jnp.concatenate([fp_ref[...], fb_ref[...]], axis=0).astype(jnp.float32)
+    quality = jnp.concatenate(
+        [quality, jnp.zeros((xs.shape[0] - top - nwin, 1), jnp.float32)], axis=0
+    )
+    white = quality * spec * lax.rsqrt(power + 1e-06)
+
+    upper = lax.broadcasted_iota(jnp.int32, (8, LANES), 0) < 4
+    for k in range(4):
+        re = white[:, k * LANES : (k + 1) * LANES]
+        im = white[:, F + k * LANES : F + (k + 1) * LANES]
+        pieces = []
+        for pair in range(nwin // 2):
+            re_p, im_p = re[pair * 8 : pair * 8 + 8], im[pair * 8 : pair * 8 + 8]
+            pieces.append(jnp.where(upper, re_p, pltpu.roll(im_p, 4, 0)))
+            pieces.append(jnp.where(upper, pltpu.roll(re_p, 4, 0), im_p))
+        pieces.append(re[top : top + 16])
+        pieces.append(im[top : top + 16])
+        slabs[k] = jnp.concatenate(pieces, axis=0).astype(jnp.bfloat16)
+    zbuf[z] = slabs[z]
+
+    def z_copy(r):
+        return pltpu.make_async_remote_copy(
+            src_ref=slabs.at[(z + r) % 4], dst_ref=zbuf.at[z],
+            send_sem=z_send.at[r - 1], recv_sem=z_recv.at[r - 1],
+            device_id=(chan, (z + r) % 4, win), device_id_type=MESH,
+        )
+
+    used = pl.ds(0, nwin * 8)
+
+    def plane_copy(d, r):
+        slot = (z + 4 - r) % 4
+        return pltpu.make_async_remote_copy(
+            src_ref=zbuf.at[slot, used], dst_ref=gath.at[d, slot],
+            send_sem=p_send.at[d, r], recv_sem=p_recv.at[d, r],
+            device_id=(flip(chan, d), z, win), device_id_type=MESH,
+        )
+
+    def relay_copy(d, r):
+        slot = (z + 4 - r) % 4
+        return pltpu.make_async_remote_copy(
+            src_ref=gath.at[d, slot], dst_ref=gath.at[d + 1, slot],
+            send_sem=p_send.at[d + 1, r], recv_sem=p_recv.at[d + 1, r],
+            device_id=(flip(chan, 1), z, win), device_id_type=MESH,
+        )
+
+    pl.semaphore_wait(barrier, 3 + len(DIRECT))
+    for r in (1, 3, 2):
+        z_copy(r).start()
+    for d in (6, 2, 4, 1):
+        plane_copy(d, 0).start()
+    last = None
+    for r in (1, 3, 2):
+        z_copy(r).wait_recv()
+        for d in (6, 2, 4, 1):
+            plane_copy(d, r).start()
+
+    for a in range(4):
+        tail = zbuf[a, top * 2 : top * 2 + 32].astype(jnp.float32) * scale
+        for w in range(nwin):
+            re_a = jnp.broadcast_to(tail[w : w + 1], (8, LANES))
+            im_a = jnp.broadcast_to(tail[16 + w : 17 + w], (8, LANES))
+            coef[0, a, w] = jnp.where(upper, re_a, im_a)
+            coef[1, a, w] = jnp.where(upper, im_a, -re_a)
+
+    for r in (0, 1, 3, 2):
+        for d in (2, 4, 6):
+            plane_copy(d, r).wait_recv()
+            relay_copy(d, r).start()
+
+    def block(read, first):
+        def pair_step(pair, carry):
+            b0 = read(pair * 2).astype(jnp.float32).reshape(nwin, 8, LANES)
+            b1 = read(pair * 2 + 1).astype(jnp.float32).reshape(nwin, 8, LANES)
+            for o in range(2):
+                for a in range(4):
+                    c = coef[o, a]
+                    p0 = jnp.sum(c * b0, axis=0)
+                    p1 = jnp.sum(c * b1, axis=0)
+                    p0 = p0 + pltpu.roll(p0, 4, 0)
+                    p1 = p1 + pltpu.roll(p1, 4, 0)
+                    start = pl.multiple_of(first + pair * 8, 8)
+                    res[o, a, pl.ds(start, 8), :] = jnp.where(upper, p0, p1)
+            return carry
+
+        lax.fori_loop(0, 2, pair_step, 0)
+
+    block(lambda k: zbuf[k, 0 : nwin * 8], chan * 16)
+    for d in (2, 4, 6, 1, 3, 5, 7):
+        if d not in DIRECT:
+            for r in range(4):
+                relay_copy(d - 1, r).wait_recv()
+        elif d == 1:
+            for r in range(4):
+                plane_copy(d, r).wait_recv()
+        block(lambda k, d=d: gath[d, k], flip(chan, d) * 16)
+
+    for o in range(2):
+        for a in range(4):
+            out_ref[o, :, a, :] = res[o, a].T
+
+    for r in (1, 2, 3):
+        z_copy(r).wait_send()
+    for r in range(4):
+        for d in DIRECT:
+            plane_copy(d, r).wait_send()
+        for d in (2, 4, 6):
+            relay_copy(d, r).wait_send()
+
+
+def fused_body(rec_block, rec_partner, flag_block, flag_partner):
+    nwin, _, samples = rec_block.shape
+    step = 1536
+    chunks = [(low, min(step, samples - low)) for low in range(0, samples, step)]
+    basis = jnp.asarray(basis_table(samples))
+    vmem = pl.BlockSpec(memory_space=pltpu.VMEM)
+    hbm = pl.BlockSpec(memory_space=pl.ANY)
+    rows = nwin * 4 + 16
+    return pl.pallas_call(
+        functools.partial(kernel, chunks, 1.0 / math.sqrt(nwin)),
+        out_shape=jax.ShapeDtypeStruct((2, LANES, 4, LANES), jnp.float32),
+        in_specs=[hbm, hbm, vmem, vmem, hbm],
+        out_specs=vmem,
+        scratch_shapes=[
+            pltpu.VMEM((nwin, samples), jnp.bfloat16),
+            pltpu.VMEM((nwin, 4, samples), jnp.bfloat16),
+            pltpu.VMEM((samples, 2 * F), jnp.bfloat16),
+            pltpu.VMEM((rows, samples), jnp.float32),
+            pltpu.VMEM((4, nwin * 8 + 32, LANES), jnp.bfloat16),
+            pltpu.VMEM((4, nwin * 8 + 32, LANES), jnp.bfloat16),
+            pltpu.VMEM((8, 4, nwin * 8, LANES), jnp.bfloat16),
+            pltpu.VMEM((2, 4, nwin, 8, LANES), jnp.float32),
+            pltpu.VMEM((2, 4, LANES, LANES), jnp.float32),
+            pltpu.SemaphoreType.DMA((2,)),
+            pltpu.SemaphoreType.DMA((len(chunks),)),
+            pltpu.SemaphoreType.DMA((3,)),
+            pltpu.SemaphoreType.DMA((3,)),
+            pltpu.SemaphoreType.DMA((8, 4)),
+            pltpu.SemaphoreType.DMA((8, 4)),
+        ],
+        compiler_params=pltpu.CompilerParams(
+            collective_id=0, has_side_effects=True, vmem_limit_bytes=40 * 1024 * 1024
+        ),
+    )(
+        rec_block.reshape(nwin, samples),
+        rec_partner,
+        flag_block.reshape(nwin, 1),
+        flag_partner.reshape(nwin * 4, 1),
+        basis,
+    )
+
+
 def solution(mesh):
     placed = (
         P("win", ("chan", "freq"), None),
@@ -77,6 +295,11 @@
         P("win", ("chan", "freq")),
         P("win", ("chan", "freq")),
     )
+    small = dict(mesh.shape) == {"chan": 8, "freq": 4, "win": 1}
     return jax.shard_map(
-        body, mesh=mesh, in_specs=placed, out_specs=P(None, "freq", "chan", "win"), check_vma=False
-    )
+        fused_body if small else body,
+        mesh=mesh,
+        in_specs=placed,
+        out_specs=P(None, "freq", "chan", "win"),
+        check_vma=False,
+    )

time: 105 us -> 28.1 us (0.27)
  other arithmetic: 56.2 us -> 0 us
  Pallas kernels: 0 us -> 18.7 us
  blocking collectives: 13.5 us -> 0 us
  local copies, waits for them, and re-layouts: 18.3 us -> 8.86 us
  starting transfers between devices: 8.73 us -> 0 us
  waiting for transfers between devices: 3.94 us -> 0 us
  matrix products: 3.31 us -> 0 us
    another operation x3 -> x0, other arithmetic: 51.8 us -> none
    pallas_call x0 -> x1, Pallas kernels: none -> 18.7 us  [fused_body(): pl.pallas_call(functools.partial(kernel, chunks, 1.0 / math.sqrt(nwin)),...]
    all_gather x1 -> x0, blocking collectives: 13.5 us -> none  [body(): lax.all_gather(partner_white, 'chan', axis=2, tiled=True)]
    all_to_all x2 -> x0, starting transfers between devices: 8.73 us -> none  [the longest x1 5.42 us: body(): lax.all_to_all(block_white, 'freq', split_axis=3, concat_axis=2, tiled=True)]
    reshape x3 -> x1, local copies, waits for them, and re-layouts: 4.36 us -> 0.07 us  [fused_body(): flag_partner.reshape(nwin * 4, 1)]
    all_to_all x2 -> x0, waiting for transfers between devices: 3.94 us -> none  [the longest x1 2.72 us: body(): lax.all_to_all(partner_white, 'freq', split_axis=3, concat_axis=2, tiled=...]
    dot_general x5 -> x0, matrix products: 3.31 us -> none  [the longest x4 2.86 us: transform(): jnp.dot(records[:, cosine_lag * extent_count:(cosine_lag + 1) * extent_co...]
    transpose x1 -> x0, other arithmetic: 2.65 us -> none  [body(): whitened = jnp.transpose(whitened, (0, 2, 1, 3))]
  transfers between devices with their start and end apart: 2 -> 0, of which waited for: 2 -> 0; matrix products, arithmetic and copies ran while one was open for 5% -> 0% of each run, Pallas kernels for 0% -> 0%
where the time goes in v1:
time: 28.1 us; the launch traced here: 27.6 us
  Pallas kernels  18.7 us (67%)
  local copies, waits for them, and re-layouts  8.86 us (32%)
    pallas_call x1, Pallas kernels, fused_body(): pl.pallas_call(functools.partial(kernel, chunks, 1.0 / math.sqrt(nwin)),...  18.7 us
    unnamed x9, local copies, waits for them, and re-layouts  8.79 us

profile of v1, /device:TPU:1, one launch (start us, length us, event | category | flops | bytes accessed | tf_op | source)
XLA Modules:
  0.0 27.6 jit_solution(2250738102327761865)
XLA Ops:
  0.0 0.7 %copy.10.fb_ref = s32[12,1]{1,0:T(8,128)S(1)} copy(s32[12,1]{0,1:T(1,128)} %param.7) | data formatting | bytes 96 | tf_op args[2]
  0.7 0.8 %copy.9 = s32[12,4]{1,0:T(8,128)S(1)} copy(s32[12,4]{0,1:T(4,128)} %param.8) | data formatting | bytes 384 | tf_op args[3]
  1.5 0.1 reshape.8.fp_ref
  1.6 0.0 copy-start
  1.6 4.5 %copy-done = bf16[6000,1024]{1,0:T(8,128)(2,1)S(1)} copy-done((bf16[6000,1024]{1,0:T(8,128)(2,1)S(1)}, bf16[6000,1024]{1,0:T(8,128)(2,1)}, u32[]{:S(2)}) %copy-start) | copy-done | bytes 12288024
  6.1 0.0 copy-start.1
  6.1 1.1 %copy-done.1 = bf16[12,4,6000]{2,1,0:T(4,128)(2,1)S(1)} copy-done((bf16[12,4,6000]{2,1,0:T(4,128)(2,1)S(1)}, bf16[12,4,6000]{2,1,0:T(4,128)(2,1)}, u32[]{:S(2)}) %copy-start.1) | copy-done | bytes 576024
  7.1 0.0 copy-start.2
  7.1 0.9 %copy-done.2 = bf16[12,1,6000]{2,0,1:T(8,128)(2,1)S(1)} copy-done((bf16[12,1,6000]{2,0,1:T(8,128)(2,1)S(1)}, bf16[12,1,6000]{2,0,1:T(8,128)(2,1)}, u32[]{:S(2)}) %copy-start.2) | copy-done | bytes 144024
  8.1 18.7 %shard_map.55 = f32[2,128,4,128]{3,2,1,0:T(4,128)S(1)} custom-call(bf16[12,6000]{1,0:T(8,128)(2,1)S(1)} %bitcast.1, bf16[12,4,6000]{2,1,0:T(4,128)(2,1)S(1)} %copy-done.1, s32[12,1]{1,0:T(8,128)S(1)} %copy.10.fb_ref, s32[48,1]{1,0:T(8,128)S(1)} %reshape.8.fp_ref, bf16[6000,1024]{1,0:T(8,128)(2,1)S(1)} %copy-done), custom_call_target="tpu_custom_call" | custom-call | tf_op jit(solution)/shard_map/pallas_call | solution.py:257
  26.8 0.8 %copy.13 = f32[2,128,4,128]{3,2,1,0:T(4,128)} copy(f32[2,128,4,128]{3,2,1,0:T(4,128)S(1)} %shard_map.55) | data formatting | bytes 1048576
Async XLA Ops:
  1.6 4.5 %copy-start = (bf16[6000,1024]{1,0:T(8,128)(2,1)S(1)}, bf16[6000,1024]{1,0:T(8,128)(2,1)}, u32[]{:S(2)}) copy-start(bf16[6000,1024]{1,0:T(8,128)(2,1)} %constant.2.clone.basis_hbm) | copy-start | bytes 36864004
  6.1 1.1 %copy-start.1 = (bf16[12,4,6000]{2,1,0:T(4,128)(2,1)S(1)}, bf16[12,4,6000]{2,1,0:T(4,128)(2,1)}, u32[]{:S(2)}) copy-start(bf16[12,4,6000]{2,1,0:T(4,128)(2,1)} %par_hbm.1) | copy-start | bytes 1728004
  7.1 0.9 %copy-start.2 = (bf16[12,1,6000]{2,0,1:T(8,128)(2,1)S(1)}, bf16[12,1,6000]{2,0,1:T(8,128)(2,1)}, u32[]{:S(2)}) copy-start(bf16[12,1,6000]{2,0,1:T(8,128)(2,1)} %param.5) | copy-start | bytes 432004

commit v2 on v1

--- a/solution.py
+++ b/solution.py
@@ -80,11 +80,22 @@
 DIRECT = (1, 2, 4, 6)
 
 
-def basis_table(samples):
-    s = np.arange(samples, dtype=np.int64)[:, None]
-    k = np.arange(F, dtype=np.int64)[None, :] + FLO
-    phase = (s * k % samples).astype(np.float64) * (2.0 * np.pi / samples)
-    return np.concatenate([np.cos(phase), -np.sin(phase)], axis=1).astype(ml_dtypes.bfloat16)
+def basis_table(samples, depth):
+    r = np.arange(samples // 4, dtype=np.int64)[:, None]
+    lane = np.arange(LANES)
+    table = np.zeros((depth, 4, 2, LANES), np.float64)
+    for m in range(4):
+        slab = (lane // 32 - m) % 4
+        k = FLO + slab * LANES + 4 * (lane % 32) + (m - FLO) % 4
+        phase = (r * k[None, :] % samples).astype(np.float64) * (2.0 * np.pi / samples)
+        table[: samples // 4, m, 0] = np.cos(phase)
+        table[: samples // 4, m, 1] = -np.sin(phase)
+    return table.reshape(depth, 8 * LANES).astype(ml_dtypes.bfloat16)
+
+
+def split(value):
+    high = value.astype(jnp.bfloat16)
+    return high, (value - high.astype(jnp.float32)).astype(jnp.bfloat16)
 
 
 def flip(chan, d):
@@ -96,7 +107,7 @@
 
 
 def kernel(
-    chunks, scale,
+    samples, scale,
     blk_hbm, par_hbm, fb_ref, fp_ref, basis_hbm, out_ref,
     blk, par, basis, xs, slabs, zbuf, gath, coef, res,
     load_sem, basis_sem, z_send, z_recv, p_send, p_recv,
@@ -108,12 +119,8 @@
     par_in = pltpu.make_async_copy(par_hbm, par, load_sem.at[1])
     blk_in.start()
     par_in.start()
-    loads = []
-    for i, (low, size) in enumerate(chunks):
-        rows = pl.ds(low, size)
-        load = pltpu.make_async_copy(basis_hbm.at[rows], basis.at[rows], basis_sem.at[i])
-        load.start()
-        loads.append(load)
+    basis_in = pltpu.make_async_copy(basis_hbm, basis, basis_sem)
+    basis_in.start()
 
     barrier = pltpu.get_barrier_semaphore()
     for r in (1, 2, 3):
@@ -121,32 +128,70 @@
     for d in DIRECT:
         pl.semaphore_signal(barrier, inc=1, device_id=(flip(chan, d), z, win), device_id_type=MESH)
 
+    rows = xs.shape[0]
+    top = nwin * 4
+    edge = samples // LANES * LANES
+    xs[:, edge:] = jnp.zeros((rows, xs.shape[1] - edge), jnp.float32)
+    xs[top + nwin :, :] = jnp.zeros((rows - top - nwin, xs.shape[1]), jnp.float32)
     par_in.wait()
     for w in range(nwin):
-        xs[w * 4 : w * 4 + 4, :] = par[w].astype(jnp.float32)
+        xs[w * 4 : w * 4 + 4, 0:samples] = par[w].astype(jnp.float32)
     blk_in.wait()
-    top = nwin * 4
-    xs[top : top + nwin, :] = blk[...].astype(jnp.float32)
-    xs[top + nwin :, :] = jnp.zeros((xs.shape[0] - top - nwin, xs.shape[1]), jnp.float32)
-
-    spec = None
-    for load, (low, size) in zip(loads, chunks):
-        load.wait()
-        x = xs[:, low : low + size].astype(jnp.bfloat16)
-        term = jnp.dot(x, basis[low : low + size, :], preferred_element_type=jnp.float32)
-        spec = term if spec is None else spec + term
-
-    power = jnp.sum(spec * spec, axis=1, keepdims=True) * (1.0 / F)
-    quality = jnp.concatenate([fp_ref[...], fb_ref[...]], axis=0).astype(jnp.float32)
-    quality = jnp.concatenate(
-        [quality, jnp.zeros((xs.shape[0] - top - nwin, 1), jnp.float32)], axis=0
-    )
-    white = quality * spec * lax.rsqrt(power + 1e-06)
+    xs[top : top + nwin, 0:samples] = blk[...].astype(jnp.float32)
+
+    quarter, depth = samples // 4, basis.shape[0]
+    x0, x1, x2, x3 = (xs[:, q * quarter : q * quarter + depth] for q in range(4))
+    even, odd = x0 + x2, x1 + x3
+    a_hi, a_lo = split(x0 - x2)
+    b_hi, b_lo = split(x1 - x3)
+    sum_hi, sum_lo = split(even + odd)
+    alt_hi, alt_lo = split(even - odd)
+    basis_in.wait()
+
+    def transform_rows(parts, m):
+        return jnp.dot(
+            jnp.concatenate(parts, axis=0),
+            basis[:, m * 2 * LANES : (m + 1) * 2 * LANES],
+            preferred_element_type=jnp.float32,
+        )
+
+    spec_re, spec_im = [], []
+    for m in range(4):
+        if m % 2 == 0:
+            got = transform_rows([sum_hi, sum_lo] if m == 0 else [alt_hi, alt_lo], m)
+            got = got[:rows] + got[rows:]
+            re, im = got[:, :LANES], got[:, LANES:]
+        else:
+            got = transform_rows([a_hi, a_lo, b_hi, b_lo], m)
+            a = got[:rows] + got[rows : 2 * rows]
+            b = got[2 * rows : 3 * rows] + got[3 * rows :]
+            sign = 1.0 if m == 1 else -1.0
+            re = a[:, :LANES] + sign * b[:, LANES:]
+            im = a[:, LANES:] - sign * b[:, :LANES]
+        spec_re.append(re)
+        spec_im.append(im)
+
+    power = sum(re * re + im * im for re, im in zip(spec_re, spec_im))
+    power = jnp.sum(power, axis=1, keepdims=True) * (1.0 / F)
+    row = lax.broadcasted_iota(jnp.int32, (rows, nwin), 0)
+    lane = lax.broadcasted_iota(jnp.int32, (rows, nwin), 1)
+    flags = jnp.concatenate(
+        [fp_ref[...].astype(jnp.float32)] * nwin
+        + [jnp.broadcast_to(fb_ref[...].astype(jnp.float32), (rows - top, nwin))],
+        axis=0,
+    )
+    window = jnp.where(row < top, row // 4, row - top)
+    quality = jnp.sum(jnp.where(lane == window, flags, 0.0), axis=1, keepdims=True)
+    weight = quality * lax.rsqrt(power + 1e-06)
 
     upper = lax.broadcasted_iota(jnp.int32, (8, LANES), 0) < 4
+    group = lax.broadcasted_iota(jnp.int32, (rows, LANES), 1) // 32
     for k in range(4):
-        re = white[:, k * LANES : (k + 1) * LANES]
-        im = white[:, F + k * LANES : F + (k + 1) * LANES]
+        re, im = spec_re[(3 - k) % 4], spec_im[(3 - k) % 4]
+        for g in range(3):
+            re = jnp.where(group == g, spec_re[(g - k) % 4], re)
+            im = jnp.where(group == g, spec_im[(g - k) % 4], im)
+        re, im = re * weight, im * weight
         pieces = []
         for pair in range(nwin // 2):
             re_p, im_p = re[pair * 8 : pair * 8 + 8], im[pair * 8 : pair * 8 + 8]
@@ -235,7 +280,9 @@
 
     for o in range(2):
         for a in range(4):
-            out_ref[o, :, a, :] = res[o, a].T
+            turned = res[o, a].T
+            for g in range(4):
+                out_ref[o, :, (g + 4 - z) % 4, a, :] = turned[g * 32 : (g + 1) * 32]
 
     for r in (1, 2, 3):
         z_copy(r).wait_send()
@@ -248,44 +295,44 @@
 
 def fused_body(rec_block, rec_partner, flag_block, flag_partner):
     nwin, _, samples = rec_block.shape
-    step = 1536
-    chunks = [(low, min(step, samples - low)) for low in range(0, samples, step)]
-    basis = jnp.asarray(basis_table(samples))
+    depth = -(-samples // 4 // LANES) * LANES
+    basis = jnp.asarray(basis_table(samples, depth))
     vmem = pl.BlockSpec(memory_space=pltpu.VMEM)
     hbm = pl.BlockSpec(memory_space=pl.ANY)
     rows = nwin * 4 + 16
-    return pl.pallas_call(
-        functools.partial(kernel, chunks, 1.0 / math.sqrt(nwin)),
-        out_shape=jax.ShapeDtypeStruct((2, LANES, 4, LANES), jnp.float32),
+    out = pl.pallas_call(
+        functools.partial(kernel, samples, 1.0 / math.sqrt(nwin)),
+        out_shape=jax.ShapeDtypeStruct((2, 32, 4, 4, LANES), jnp.float32),
         in_specs=[hbm, hbm, vmem, vmem, hbm],
         out_specs=vmem,
         scratch_shapes=[
             pltpu.VMEM((nwin, samples), jnp.bfloat16),
             pltpu.VMEM((nwin, 4, samples), jnp.bfloat16),
-            pltpu.VMEM((samples, 2 * F), jnp.bfloat16),
-            pltpu.VMEM((rows, samples), jnp.float32),
+            pltpu.VMEM((depth, 2 * F), jnp.bfloat16),
+            pltpu.VMEM((rows, samples // LANES * LANES + 2 * LANES), jnp.float32),
             pltpu.VMEM((4, nwin * 8 + 32, LANES), jnp.bfloat16),
             pltpu.VMEM((4, nwin * 8 + 32, LANES), jnp.bfloat16),
             pltpu.VMEM((8, 4, nwin * 8, LANES), jnp.bfloat16),
             pltpu.VMEM((2, 4, nwin, 8, LANES), jnp.float32),
             pltpu.VMEM((2, 4, LANES, LANES), jnp.float32),
             pltpu.SemaphoreType.DMA((2,)),
-            pltpu.SemaphoreType.DMA((len(chunks),)),
+            pltpu.SemaphoreType.DMA,
             pltpu.SemaphoreType.DMA((3,)),
             pltpu.SemaphoreType.DMA((3,)),
             pltpu.SemaphoreType.DMA((8, 4)),
             pltpu.SemaphoreType.DMA((8, 4)),
         ],
         compiler_params=pltpu.CompilerParams(
-            collective_id=0, has_side_effects=True, vmem_limit_bytes=40 * 1024 * 1024
+            collective_id=0, has_side_effects=True, vmem_limit_bytes=60 * 1024 * 1024
         ),
     )(
         rec_block.reshape(nwin, samples),
         rec_partner,
-        flag_block.reshape(nwin, 1),
-        flag_partner.reshape(nwin * 4, 1),
+        flag_block.T,
+        flag_partner.T,
         basis,
     )
+    return out.reshape(2, LANES, 4, LANES)
 
 
 def solution(mesh):

time: 28.1 us -> 21.4 us (0.76)
  local copies, waits for them, and re-layouts: 8.86 us -> 1.87 us
  Pallas kernels: 18.7 us -> 19.1 us
    unnamed x9 -> x1, local copies, waits for them, and re-layouts: 8.79 us -> 1.87 us
    pallas_call x1, Pallas kernels: 18.7 us -> 19.1 us  [fused_body(): pl.pallas_call(functools.partial(kernel, samples, 1.0 / math.sqrt(nwin)),...]
where the time goes in v2:
time: 21.4 us; the launch traced here: 21 us
  Pallas kernels  19.1 us (89%)
  local copies, waits for them, and re-layouts  1.87 us (9%)
    pallas_call x1, Pallas kernels, fused_body(): pl.pallas_call(functools.partial(kernel, samples, 1.0 / math.sqrt(nwin)),...  19.1 us
    unnamed x1, local copies, waits for them, and re-layouts  1.87 us

profile of v2, /device:TPU:1, one launch (start us, length us, event | category | flops | bytes accessed | tf_op | source)
XLA Modules:
  0.0 21.0 jit_solution(8451310104158029128)
XLA Ops:
  0.0 19.1 %shard_map.55 = f32[2,32,4,4,128]{4,3,2,1,0:T(4,128)} custom-call(bf16[12,6000]{1,0:T(8,128)(2,1)} %bitcast.5, bf16[12,4,6000]{2,1,0:T(4,128)(2,1)} %par_hbm.1, s32[1,12]{1,0:T(1,128)} %bitcast.7, s32[4,12]{1,0:T(4,128)} %bitcast.6, bf16[1536,1024]{1,0:T(8,128)(2,1)} %constant.2.clone.basis_hbm), custom_call_target="tpu_custom_call" | custom-call | tf_op jit(solution)/shard_map/pallas_call | solution.py:303
  19.1 1.9 %copy.7 = f32[2,128,4,128]{3,2,1,0:T(4,128)} copy(f32[2,128,4,128]{3,2,1,0:T(4,128)} %bitcast.4) | data formatting | bytes 1048576

commit v3 on v2

--- a/solution.py
+++ b/solution.py
@@ -77,6 +77,7 @@
 
 MESH = pl.DeviceIdType.MESH
 LANES = 128
+ORDER = (0, 1, 3, 2)
 DIRECT = (1, 2, 4, 6)
 
 
@@ -228,15 +229,21 @@
         )
 
     pl.semaphore_wait(barrier, 3 + len(DIRECT))
-    for r in (1, 3, 2):
+    for r in ORDER[1:]:
         z_copy(r).start()
     for d in (6, 2, 4, 1):
         plane_copy(d, 0).start()
-    last = None
-    for r in (1, 3, 2):
+    for r in ORDER[1:]:
         z_copy(r).wait_recv()
         for d in (6, 2, 4, 1):
             plane_copy(d, r).start()
+
+    def relay(r):
+        for d in (2, 4, 6):
+            plane_copy(d, r).wait_recv()
+            relay_copy(d, r).start()
+
+    relay(0)
 
     for a in range(4):
         tail = zbuf[a, top * 2 : top * 2 + 32].astype(jnp.float32) * scale
@@ -246,37 +253,38 @@
             coef[0, a, w] = jnp.where(upper, re_a, im_a)
             coef[1, a, w] = jnp.where(upper, im_a, -re_a)
 
-    for r in (0, 1, 3, 2):
+    half = lax.broadcasted_iota(jnp.int32, (8, LANES), 0) // 4
+
+    def piece(data, d, r):
+        slot = (z + 4 - r) % 4
+        b = data.astype(jnp.float32).reshape(nwin, 8, LANES)
+        start = pl.multiple_of(flip(chan, d) * 16 + slot // 2 * 8, 8)
+        mine = half == slot % 2
+        for o in range(2):
+            for a in range(4):
+                p = jnp.sum(coef[o, a] * b, axis=0)
+                p = p + pltpu.roll(p, 4, 0)
+                old = res[o, a, pl.ds(start, 8), :]
+                res[o, a, pl.ds(start, 8), :] = jnp.where(mine, p, old)
+
+    def held(d, r):
+        return gath[d, (z + 4 - r) % 4]
+
+    for r in range(4):
+        if r:
+            relay(ORDER[r])
+        piece(zbuf[(z + 4 - ORDER[r]) % 4, 0 : nwin * 8], 0, ORDER[r])
+        plane_copy(1, ORDER[r]).wait_recv()
+        piece(held(1, ORDER[r]), 1, ORDER[r])
         for d in (2, 4, 6):
-            plane_copy(d, r).wait_recv()
-            relay_copy(d, r).start()
-
-    def block(read, first):
-        def pair_step(pair, carry):
-            b0 = read(pair * 2).astype(jnp.float32).reshape(nwin, 8, LANES)
-            b1 = read(pair * 2 + 1).astype(jnp.float32).reshape(nwin, 8, LANES)
-            for o in range(2):
-                for a in range(4):
-                    c = coef[o, a]
-                    p0 = jnp.sum(c * b0, axis=0)
-                    p1 = jnp.sum(c * b1, axis=0)
-                    p0 = p0 + pltpu.roll(p0, 4, 0)
-                    p1 = p1 + pltpu.roll(p1, 4, 0)
-                    start = pl.multiple_of(first + pair * 8, 8)
-                    res[o, a, pl.ds(start, 8), :] = jnp.where(upper, p0, p1)
-            return carry
-
-        lax.fori_loop(0, 2, pair_step, 0)
-
-    block(lambda k: zbuf[k, 0 : nwin * 8], chan * 16)
-    for d in (2, 4, 6, 1, 3, 5, 7):
-        if d not in DIRECT:
-            for r in range(4):
-                relay_copy(d - 1, r).wait_recv()
-        elif d == 1:
-            for r in range(4):
-                plane_copy(d, r).wait_recv()
-        block(lambda k, d=d: gath[d, k], flip(chan, d) * 16)
+            piece(held(d, ORDER[r]), d, ORDER[r])
+        if r:
+            for d in (2, 4, 6):
+                relay_copy(d, ORDER[r - 1]).wait_recv()
+                piece(held(d + 1, ORDER[r - 1]), d + 1, ORDER[r - 1])
+    for d in (2, 4, 6):
+        relay_copy(d, ORDER[3]).wait_recv()
+        piece(held(d + 1, ORDER[3]), d + 1, ORDER[3])
 
     for o in range(2):
         for a in range(4):

time: 21.4 us -> 21.3 us (level)
  no operation moved by 1% of the time
where the time goes in v3:
time: 21.3 us; the launch traced here: 20.9 us
  Pallas kernels  19 us (89%)
  local copies, waits for them, and re-layouts  1.87 us (9%)
    pallas_call x1, Pallas kernels, fused_body(): pl.pallas_call(functools.partial(kernel, samples, 1.0 / math.sqrt(nwin)),...  19 us
    unnamed x1, local copies, waits for them, and re-layouts  1.87 us

profile of v3, /device:TPU:1, one launch (start us, length us, event | category | flops | bytes accessed | tf_op | source)
XLA Modules:
  0.0 20.9 jit_solution(17955728844965998521)
XLA Ops:
  0.0 19.0 %shard_map.55 = f32[2,32,4,4,128]{4,3,2,1,0:T(4,128)} custom-call(bf16[12,6000]{1,0:T(8,128)(2,1)} %bitcast.5, bf16[12,4,6000]{2,1,0:T(4,128)(2,1)} %par_hbm.1, s32[1,12]{1,0:T(1,128)} %bitcast.7, s32[4,12]{1,0:T(4,128)} %bitcast.6, bf16[1536,1024]{1,0:T(8,128)(2,1)} %constant.2.clone.basis_hbm), custom_call_target="tpu_custom_call" | custom-call | tf_op jit(solution)/shard_map/pallas_call | solution.py:311
  19.0 1.9 %copy.7 = f32[2,128,4,128]{3,2,1,0:T(4,128)} copy(f32[2,128,4,128]{3,2,1,0:T(4,128)} %bitcast.4) | data formatting | bytes 1048576

commit v4 on v3

--- a/solution.py
+++ b/solution.py
@@ -77,7 +77,7 @@
 
 MESH = pl.DeviceIdType.MESH
 LANES = 128
-ORDER = (0, 1, 3, 2)
+ORDER = (0, 1, 2, 3)
 DIRECT = (1, 2, 4, 6)
 
 
@@ -107,6 +107,13 @@
     return core + 2 * x + 4 * y
 
 
+def across(z, r):
+    low, high = z % 2, z // 2
+    low = 1 - low if r & 1 else low
+    high = 1 - high if r & 2 else high
+    return low + 2 * high
+
+
 def kernel(
     samples, scale,
     blk_hbm, par_hbm, fb_ref, fp_ref, basis_hbm, out_ref,
@@ -125,7 +132,7 @@
 
     barrier = pltpu.get_barrier_semaphore()
     for r in (1, 2, 3):
-        pl.semaphore_signal(barrier, inc=1, device_id=(chan, (z + r) % 4, win), device_id_type=MESH)
+        pl.semaphore_signal(barrier, inc=1, device_id=(chan, across(z, r), win), device_id_type=MESH)
     for d in DIRECT:
         pl.semaphore_signal(barrier, inc=1, device_id=(flip(chan, d), z, win), device_id_type=MESH)
 
@@ -205,15 +212,15 @@
 
     def z_copy(r):
         return pltpu.make_async_remote_copy(
-            src_ref=slabs.at[(z + r) % 4], dst_ref=zbuf.at[z],
+            src_ref=slabs.at[across(z, r)], dst_ref=zbuf.at[z],
             send_sem=z_send.at[r - 1], recv_sem=z_recv.at[r - 1],
-            device_id=(chan, (z + r) % 4, win), device_id_type=MESH,
+            device_id=(chan, across(z, r), win), device_id_type=MESH,
         )
 
     used = pl.ds(0, nwin * 8)
 
     def plane_copy(d, r):
-        slot = (z + 4 - r) % 4
+        slot = across(z, r)
         return pltpu.make_async_remote_copy(
             src_ref=zbuf.at[slot, used], dst_ref=gath.at[d, slot],
             send_sem=p_send.at[d, r], recv_sem=p_recv.at[d, r],
@@ -221,7 +228,7 @@
         )
 
     def relay_copy(d, r):
-        slot = (z + 4 - r) % 4
+        slot = across(z, r)
         return pltpu.make_async_remote_copy(
             src_ref=gath.at[d, slot], dst_ref=gath.at[d + 1, slot],
             send_sem=p_send.at[d + 1, r], recv_sem=p_recv.at[d + 1, r],
@@ -256,7 +263,7 @@
     half = lax.broadcasted_iota(jnp.int32, (8, LANES), 0) // 4
 
     def piece(data, d, r):
-        slot = (z + 4 - r) % 4
+        slot = across(z, r)
         b = data.astype(jnp.float32).reshape(nwin, 8, LANES)
         start = pl.multiple_of(flip(chan, d) * 16 + slot // 2 * 8, 8)
         mine = half == slot % 2
@@ -268,12 +275,12 @@
                 res[o, a, pl.ds(start, 8), :] = jnp.where(mine, p, old)
 
     def held(d, r):
-        return gath[d, (z + 4 - r) % 4]
+        return gath[d, across(z, r)]
 
     for r in range(4):
         if r:
             relay(ORDER[r])
-        piece(zbuf[(z + 4 - ORDER[r]) % 4, 0 : nwin * 8], 0, ORDER[r])
+        piece(zbuf[across(z, ORDER[r]), 0 : nwin * 8], 0, ORDER[r])
         plane_copy(1, ORDER[r]).wait_recv()
         piece(held(1, ORDER[r]), 1, ORDER[r])
         for d in (2, 4, 6):

time: 21.3 us -> 20.7 us (0.972); the launches traced: 20.9 us -> 20.5 us
  Pallas kernels: 19 us -> 18.6 us
    pallas_call x1, Pallas kernels: 19 us -> 18.6 us  [fused_body(): pl.pallas_call(functools.partial(kernel, samples, 1.0 / math.sqrt(nwin)),...]
where the time goes in v4:
time: 20.7 us; the launch traced here: 20.5 us
  Pallas kernels  18.6 us (90%)
  local copies, waits for them, and re-layouts  1.87 us (9%)
    pallas_call x1, Pallas kernels, fused_body(): pl.pallas_call(functools.partial(kernel, samples, 1.0 / math.sqrt(nwin)),...  18.6 us
    unnamed x1, local copies, waits for them, and re-layouts  1.87 us

profile of v4, /device:TPU:1, one launch (start us, length us, event | category | flops | bytes accessed | tf_op | source)
XLA Modules:
  0.0 20.5 jit_solution(4019316502595898043)
XLA Ops:
  0.0 18.6 %shard_map.55 = f32[2,32,4,4,128]{4,3,2,1,0:T(4,128)} custom-call(bf16[12,6000]{1,0:T(8,128)(2,1)} %bitcast.5, bf16[12,4,6000]{2,1,0:T(4,128)(2,1)} %par_hbm.1, s32[1,12]{1,0:T(1,128)} %bitcast.7, s32[4,12]{1,0:T(4,128)} %bitcast.6, bf16[1536,1024]{1,0:T(8,128)(2,1)} %constant.2.clone.basis_hbm), custom_call_target="tpu_custom_call" | custom-call | tf_op jit(solution)/shard_map/pallas_call | solution.py:318
  18.7 1.9 %copy.7 = f32[2,128,4,128]{3,2,1,0:T(4,128)} copy(f32[2,128,4,128]{3,2,1,0:T(4,128)} %bitcast.4) | data formatting | bytes 1048576
